TPU v7x, 512 devices: a whole 4x8x8 slice. The times are simulated.
512 devices in a mesh: dp: 2 (over x_lo), row: 8 (over z), col: 32 (over y, x_hi, core).
Axes of the slice: x: 4 (x_hi: 2, x_lo: 2; x = x_hi * 2 + x_lo), y: 8, z: 8, core: 2. Of those that a mesh axis runs over, the one named last changes fastest.
Arguments:
- tokens: bfloat16 [512, 8192], P(('dp', 'col'), 'row'), may hold values from -6 to 6
- gate_weight: bfloat16 [8192, 14336], P('row', 'col'), may hold values from -0.0625 to 0.0625
- up_weight: bfloat16 [8192, 14336], P('row', 'col'), may hold values from -0.0625 to 0.0625
- down_weight: bfloat16 [14336, 8192], P('col', 'row'), may hold values from -0.046875 to 0.046875
- cotangent: bfloat16 [512, 8192], P(('dp', 'col'), 'row'), may hold values from -6 to 6
Outputs:
- layer_output: bfloat16 [512, 8192], P(('dp', 'col'), 'row')
- grad_input: bfloat16 [512, 8192], P(('dp', 'col'), 'row')
- grad_gate: bfloat16 [8192, 14336], P('row', 'col')
- grad_up: bfloat16 [8192, 14336], P('row', 'col')
All inputs are finite; a program needn't handle non-finite values.
Results may differ from a plain program's by a relative error of at most 0.02.
Values may be sent and summed in bfloat16 or wider, within the bound.
A program may use at most 64 MiB of HBM per device.

v0:
```python
import jax
import jax.numpy as jnp
from jax import lax
from jax.sharding import PartitionSpec as P


def times_transpose(left, right):
    return lax.dot_general(
        left, right, (((1,), (1,)), ((), ())), preferred_element_type=jnp.float32
    )


def over_tokens(left, right):
    return lax.dot_general(
        left, right, (((0,), (0,)), ((), ())), preferred_element_type=jnp.float32
    )


def local_grads(activations, grad_gate_rows, grad_up_rows):
    return (
        over_tokens(activations, grad_gate_rows).astype(jnp.bfloat16),
        over_tokens(activations, grad_up_rows).astype(jnp.bfloat16),
    )


def body(tokens, gate_weight, up_weight, down_weight, cotangent):
    hidden_width = gate_weight.shape[1]
    gathered = lax.all_gather(tokens, "col", axis=0, tiled=True)
    row_block = gathered
    joined = lax.psum_scatter(
        jnp.concatenate(
            [
                jnp.dot(row_block, gate_weight, preferred_element_type=jnp.float32),
                jnp.dot(row_block, up_weight, preferred_element_type=jnp.float32),
            ],
            axis=1,
        ),
        "row",
        scatter_dimension=0,
        tiled=True,
    )
    gate_pre = joined[:, :hidden_width]
    up_pre = joined[:, hidden_width:]
    silu_gate = jax.nn.silu(gate_pre)
    hidden = (silu_gate * up_pre).astype(jnp.bfloat16)
    hidden_all = lax.all_gather(hidden, "row", axis=0, tiled=True)
    row_block = hidden_all
    layer_output = lax.psum_scatter(
        jnp.dot(row_block, down_weight, preferred_element_type=jnp.float32),
        "col",
        scatter_dimension=0,
        tiled=True,
    ).astype(jnp.bfloat16)
    back_rows = lax.all_gather(cotangent, "col", axis=0, tiled=True)
    row_block = back_rows
    grad_hidden = lax.psum_scatter(
        times_transpose(row_block, down_weight), "row", scatter_dimension=0, tiled=True
    )
    sigmoid_gate = jax.nn.sigmoid(gate_pre)
    grad_gate_pre = (
        grad_hidden * up_pre * sigmoid_gate * (1.0 + gate_pre * (1.0 - sigmoid_gate))
    ).astype(jnp.bfloat16)
    grad_up_pre = (grad_hidden * silu_gate).astype(jnp.bfloat16)
    gate_rows_all, up_rows_all = (
        lax.all_gather(grad_gate_pre, "row", axis=0, tiled=True),
        lax.all_gather(grad_up_pre, "row", axis=0, tiled=True),
    )
    grad_input = lax.psum_scatter(
        (
            times_transpose(gate_rows_all, gate_weight) + times_transpose(up_rows_all, up_weight)
        ).astype(jnp.bfloat16),
        "col",
        scatter_dimension=0,
        tiled=True,
    )
    own_grads = local_grads(gathered, gate_rows_all, up_rows_all)
    total_gate, total_up = (
        lax.psum(own_grads[0], "dp").astype(jnp.float32),
        lax.psum(own_grads[1], "dp").astype(jnp.float32),
    )
    return (
        layer_output,
        grad_input,
        total_gate.astype(jnp.bfloat16),
        total_up.astype(jnp.bfloat16),
    )


def solution(mesh):
    return jax.shard_map(
        body,
        mesh=mesh,
        in_specs=(
            P(("dp", "col"), "row"),
            P("row", "col"),
            P("row", "col"),
            P("col", "row"),
            P(("dp", "col"), "row"),
        ),
        out_specs=(
            P(("dp", "col"), "row"),
            P(("dp", "col"), "row"),
            P("row", "col"),
            P("row", "col"),
        ),
        check_vma=False,
    )
```

profile of v0, /device:TPU:1, one launch (start us, length us, event | category | flops | bytes accessed | tf_op | source)
XLA Modules:
  0.0 499.5 jit_solution(6677779627938258308)
XLA Ops:
  7.2 45.4 %all_gather.17 = bf16[256,1024]{1,0:T(8,128)(2,1)S(1)} all-gather(bf16[8,1024]{1,0:T(8,128)(2,1)} %param.9), channel_id=1, replica_groups=mesh['dp'=2,'row'=8,'col'=32] {'col'}, dimensions={0}, use_global_device_ids=true | all-gather | bytes 540672 | tf_op jit(solution)/shard_map/all_gather | solution.py:54
  52.7 1.3 fusion.7
  54.0 40.8 %all_gather.15 = bf16[256,1024]{1,0:T(8,128)(2,1)S(1)} all-gather(bf16[8,1024]{1,0:T(8,128)(2,1)S(1)} %copy-done.7), channel_id=1, replica_groups=mesh['dp'=2,'row'=8,'col'=32] {'col'}, dimensions={0}, use_global_device_ids=true | all-gather | bytes 540672 | tf_op jit(solution)/shard_map/all_gather | solution.py:28
  94.8 0.4 fusion.5
  95.2 0.7 copy-done.1
  96.0 0.4 fusion.4
  96.5 1.2 copy.20
  97.8 36.1 %reduce-scatter.13.cloned.1.call-done = f32[32,896]{1,0:T(8,128)} async-done(((f32[256,896]{1,0:T(8,128)}), f32[32,896]{1,0:T(8,128)}) %reduce-scatter.13.cloned.1.call-update) | async-done | bytes 114704 | tf_op jit(solution)/shard_map/reduce_scatter | solution.py:30
  133.9 1.0 multiply_convert_fusion
  134.9 18.8 %all_gather.16 = bf16[256,448]{1,0:T(8,128)(2,1)S(1)} all-gather(bf16[32,448]{1,0:T(8,128)(2,1)S(1)} %get-tuple-element.8), channel_id=1, replica_groups=mesh['dp'=2,'row'=8,'col'=32] {'row'}, dimensions={0}, use_global_device_ids=true | all-gather | bytes 258048 | tf_op jit(solution)/shard_map/all_gather | solution.py:46
  153.7 1.4 fusion.6
  155.2 18.6 %all_gather.18 = bf16[256,448]{1,0:T(8,128)(2,1)S(1)} all-gather(bf16[32,448]{1,0:T(8,128)(2,1)S(1)} %get-tuple-element.7), channel_id=1, replica_groups=mesh['dp'=2,'row'=8,'col'=32] {'row'}, dimensions={0}, use_global_device_ids=true | all-gather | bytes 258048 | tf_op jit(solution)/shard_map/all_gather | solution.py:65
  173.8 18.4 %all_gather.19 = bf16[256,448]{1,0:T(8,128)(2,1)S(1)} all-gather(bf16[32,448]{1,0:T(8,128)(2,1)S(1)} %get-tuple-element.6), channel_id=1, replica_groups=mesh['dp'=2,'row'=8,'col'=32] {'row'}, dimensions={0}, use_global_device_ids=true | all-gather | bytes 258048 | tf_op jit(solution)/shard_map/all_gather | solution.py:66
  192.3 0.4 fusion.8
  193.0 0.6 copy-done.3
  193.5 1.2 fusion.2
  194.8 1.3 fusion
  196.2 1.3 fusion.1
  197.6 84.2 %reduce-scatter.9.cloned.1.call-done = f32[8,1024]{1,0:T(8,128)} async-done(((f32[256,1024]{1,0:T(8,128)}), f32[8,1024]{1,0:T(8,128)}) %reduce-scatter.9.cloned.1.call-update) | async-done | bytes 32784 | tf_op jit(solution)/shard_map/reduce_scatter | solution.py:48
  281.8 1.4 convert_element_type.32
  283.1 124.7 %reduce-scatter.11.cloned.1.call-done = bf16[8,1024]{1,0:T(8,128)(2,1)} async-done(((bf16[256,1024]{1,0:T(8,128)(2,1)}), bf16[8,1024]{1,0:T(8,128)(2,1)}) %reduce-scatter.11.cloned.1.call-update) | async-done | bytes 16400 | tf_op jit(solution)/shard_map/reduce_scatter | solution.py:68
  407.8 82.0 %all-reduce.3.cloned.1.call-done = (bf16[1024,448]{0,1:T(8,128)(2,1)}, bf16[1024,448]{0,1:T(8,128)(2,1)}) async-done(((bf16[1024,448]{0,1:T(8,128)(2,1)}, bf16[1024,448]{0,1:T(8,128)(2,1)}), (bf16[1024,448]{0,1:T(8,128)(2,1)}, bf16[1024,448]{0,1:T(8,128)(2,1)})) %all-reduce.3.cloned.1.call-update) | async-done | bytes 1835024 | tf_op jit(solution)/shard_map/psum | solution.py:78
  489.8 2.2 copy.26
  492.0 0.9 copy.27
  (26 shorter events, 0.7 us)
Async XLA Ops:
  7.2 45.5 %copy-start = (bf16[448,1024]{1,0:T(8,128)(2,1)S(1)}, bf16[448,1024]{1,0:T(8,128)(2,1)}, u32[]{:S(2)}) copy-start(bf16[448,1024]{1,0:T(8,128)(2,1)} %param.8) | copy-start | bytes 2752516
  7.2 90.6 %reduce-scatter.15.cloned.1.call-start = ((), (), s32[]{:S(2)}) async-start(), calls=%async_computation.7 | async-start | bytes 589824 | tf_op jit(solution)/shard_map/reduce_scatter | solution.py:56
  52.7 1.3 copy-start.7
  52.7 42.1 %copy-start.2 = (bf16[1024,448]{0,1:T(8,128)(2,1)S(1)}, bf16[1024,448]{0,1:T(8,128)(2,1)}, u32[]{:S(2)}) copy-start(bf16[1024,448]{0,1:T(8,128)(2,1)} %param.7) | copy-start | bytes 2752516
  54.0 79.9 %reduce-scatter.13.cloned.1.call-start = ((), (), s32[]{:S(2)}) async-start(), calls=%async_computation.6 | async-start | bytes 1032192 | tf_op jit(solution)/shard_map/reduce_scatter | solution.py:30
  94.8 1.2 copy-start.1
  97.7 184.1 %reduce-scatter.9.cloned.1.call-start = ((), (), s32[]{:S(2)}) async-start(), calls=%async_computation.4 | async-start | bytes 1081344 | tf_op jit(solution)/shard_map/reduce_scatter | solution.py:48
  155.1 252.7 %reduce-scatter.11.cloned.1.call-start = ((), (), s32[]{:S(2)}) async-start(), calls=%async_computation.5 | async-start | bytes 540672 | tf_op jit(solution)/shard_map/reduce_scatter | solution.py:68
  192.2 0.7 copy-start.4
  192.2 1.3 copy-start.3
  194.8 1.4 copy-start.5
  194.8 295.0 %all-reduce.3.cloned.1.call-start = ((), (), s32[]{:S(2)}) async-start(), calls=%async_computation.8 | async-start | bytes 3670016 | tf_op jit(solution)/shard_map/psum | solution.py:78
  489.8 2.2 copy-start.6
Sparse Core Ops, SparseCore 0:
  54.1 35.4 reduce-scatter.14
  97.8 35.9 reduce-scatter.12
  155.3 126.4 reduce-scatter.8
  287.5 120.2 reduce-scatter.10
  411.1 78.5 all-reduce.2
where the time goes:
time: 500 us; the launch traced here: 499 us
  waiting for transfers between devices  327 us (65%)
  blocking collectives  142 us (28%)
  between operations  13.8 us (3%)
  matrix products  7.93 us (2%)
  local copies, waits for them, and re-layouts  5.99 us (1%)
    reduce_scatter x1, waiting for transfers between devices, body(): lax.psum_scatter((times_transpose(gate_rows_all, gate_weight) + times_tra...  125 us
    reduce_scatter x1, waiting for transfers between devices, body(): lax.psum_scatter(jnp.dot(row_block, down_weight, preferred_element_type=j...  84.2 us
    psum x1, waiting for transfers between devices, body(): lax.psum(own_grads[0], 'dp').astype(jnp.float32)  82 us
    all_gather x1, blocking collectives, body(): back_rows = lax.all_gather(cotangent, 'col', axis=0, tiled=True)  45.4 us
    all_gather x1, blocking collectives, body(): gathered = lax.all_gather(tokens, 'col', axis=0, tiled=True)  40.8 us
    reduce_scatter x1, waiting for transfers between devices, body(): lax.psum_scatter(jnp.concatenate([jnp.dot(row_block, gate_weight, preferr...  36.1 us
    all_gather x1, blocking collectives, body(): hidden_all = lax.all_gather(hidden, 'row', axis=0, tiled=True)  18.8 us
    all_gather x1, blocking collectives, body(): lax.all_gather(grad_gate_pre, 'row', axis=0, tiled=True)  18.6 us
  transfers between devices with their start and end apart: 5, of which 4 were waited for; matrix products, arithmetic and copies ran while one was open for 2% of the time, Pallas kernels for 0%

commit v1 on v0

v1 whole, which is shorter than its diff:
```python
import functools

import jax
import jax.numpy as jnp
from jax import lax
from jax.experimental import pallas as pl
from jax.experimental.pallas import tpu as pltpu
from jax.sharding import PartitionSpec as P

MESH = pl.DeviceIdType.MESH
F32, BF16 = jnp.float32, jnp.bfloat16

GROUPS = {}
N_SEM = 0
for _name, _count in (
    ("tok", 16), ("cot", 16), ("tok_sib", 2), ("cot_sib", 2), ("zgu", 8), ("zgh", 8), ("agu", 8), ("agh", 8),
    ("px", 1), ("pu", 1), ("ph", 1), ("lo_sib", 1), ("gi_sib", 1), ("lo", 16), ("gi", 16),
):
    GROUPS[_name] = N_SEM
    N_SEM += _count


def dot(a, b):
    return lax.dot_general(a, b, (((1,), (0,)), ((), ())), preferred_element_type=F32)


def dot_nt(a, b):
    return lax.dot_general(a, b, (((1,), (1,)), ((), ())), preferred_element_type=F32)


def dot_tn(a, b):
    return lax.dot_general(a, b, (((0,), (0,)), ((), ())), preferred_element_type=F32)


def join(a, b):
    return jnp.concatenate([a[:, :384], b[:, :384], a[:, 384:], b[:, 384:]], axis=1)


def part(x):
    tail = x[:, 768:896]
    return (
        jnp.concatenate([x[:, :384], tail], axis=1),
        jnp.concatenate([x[:, 384:768], pltpu.roll(tail, 64, 1)], axis=1),
    )


def fold(x):
    return jnp.concatenate([x[:, :512], x[:, 512:]], axis=0)


def kernel(
    tok_ref, wg_hbm, wu_hbm, wd_hbm, cot_ref,
    lo_out, gi_out, gg_out, gu_out,
    wg, wu, wd, gx, gc, x, cx, px, sgu, rgu, sgh, rgh, agu, agh, pu, ph,
    hid, gg, gu, part_f, lo_s, lo_i, gi_s, gi_i, lo_t, lo_r, gi_t, gi_r,
    send, recv, wsem,
):
    dp, r, c = lax.axis_index("dp"), lax.axis_index("row"), lax.axis_index("col")
    k = lax.rem(c, 2)
    xh = lax.rem(c // 2, 2)
    y = c // 4
    sib = (dp, r, c + 1 - 2 * k)
    peer = (1 - dp, r, c)
    my_q = r // 2 + 4 * lax.rem(r, 2)

    def chip(j):
        q, dx = j // 2, lax.rem(j, 2)
        odd = lax.rem(q, 2)
        dy = odd * ((q + 1) // 2) + (1 - odd) * (8 - q // 2)
        back = jnp.where(q == 0, 0, jnp.where(q == 7, 7, q - 1 + 2 * odd))
        to = (lax.rem(y + dy, 8) * 2 + lax.rem(xh + dx, 2)) * 2 + k
        return (dp, r, to), back * 2 + dx

    def ring(i):
        odd = lax.rem(i, 2)
        return lax.rem(r + odd * ((i + 1) // 2) + (1 - odd) * (8 - i // 2), 8)

    def copy(src, dst, s, d, to):
        return pltpu.make_async_remote_copy(
            src_ref=src, dst_ref=dst, send_sem=send.at[s], recv_sem=recv.at[d], device_id=to, device_id_type=MESH
        )

    def arrived(dst, d):
        pltpu.make_async_copy(dst, dst, recv.at[d]).wait()

    def left(src, s):
        pltpu.make_async_copy(src, src, send.at[s]).wait()

    def loop(lo, hi, body):
        def step(i, carry):
            body(i)
            return carry
        lax.fori_loop(lo, hi, step, 0)

    loads = [
        pltpu.make_async_copy(a, b, wsem.at[i]) for i, (a, b) in enumerate(((wg_hbm, wg), (wu_hbm, wu), (wd_hbm, wd)))
    ]
    for load in loads:
        load.start()

    barrier = pltpu.get_barrier_semaphore()

    def greet(to):
        pl.semaphore_signal(barrier, inc=1, device_id=to, device_id_type=MESH)

    loop(1, 16, lambda j: greet(chip(j)[0]))
    loop(1, 8, lambda i: greet((dp, ring(i), c)))
    greet(sib)
    greet(peer)
    gx[k, 0] = fold(tok_ref[...].astype(F32)).astype(BF16)
    gc[k, 0] = fold(cot_ref[...].astype(F32)).astype(BF16)
    pl.semaphore_wait(barrier, 24)

    def spread(buf, base):
        def one(j):
            to, slot = chip(j)
            copy(buf.at[k, 0], buf.at[k, slot], base + j, base + slot, to).start()
        loop(1, 16, one)

    spread(gx, GROUPS["tok"])
    spread(gc, GROUPS["cot"])

    def collect(buf, rows, half, base, sib_base):
        lo = 8 * half
        loop(max(lo, 1), lo + 8, lambda j: arrived(buf.at[k, j], base + j))
        mine = buf.at[k, pl.ds(lo, 8)]
        copy(mine, mine, sib_base + half, sib_base + half, sib).start()
        theirs = buf.at[1 - k, pl.ds(lo, 8)]
        arrived(theirs, sib_base + half)

        def unfold(q):
            for core in range(2):
                a, b = buf[core, 2 * q].astype(F32), buf[core, 2 * q + 1].astype(F32)
                left_half = jnp.concatenate([a[:8], b[:8]], axis=0)
                right_half = jnp.concatenate([a[8:], b[8:]], axis=0)
                at = pl.ds(pl.multiple_of(32 * q + 16 * core, 16), 16)
                rows[at, :512] = left_half.astype(BF16)
                rows[at, 512:] = right_half.astype(BF16)
        loop(4 * half, 4 * half + 4, unfold)

    def scatter(src, dst, half, base):
        def one(i):
            to = lax.rem((r // 2) * 2 + 2 * i + half, 8)

            @pl.when(to != r)
            def _():
                copy(src.at[to], dst.at[r], base + to, base + r, (dp, to, c)).start()

            @pl.when(to == r)
            def _():
                dst[r] = src[r]
        loop(0, 4, one)

    for half in range(2):
        collect(gx, x, half, GROUPS["tok"], GROUPS["tok_sib"])
        if half == 0:
            loads[0].wait()
            loads[1].wait()
        lhs = x[128 * half:128 * half + 128]
        gate, up = dot(lhs, wg[...]), dot(lhs, wu[...])
        for i in range(4):
            at = slice(32 * i, 32 * i + 32)
            sgu[2 * i + half] = join(gate[at], up[at]).astype(BF16)
        scatter(sgu, rgu, half, GROUPS["zgu"])
    copy(x, px, GROUPS["px"], GROUPS["px"], peer).start()
    for half in range(2):
        collect(gc, cx, half, GROUPS["cot"], GROUPS["cot_sib"])
        if half == 0:
            loads[2].wait()
        back = dot_nt(cx[128 * half:128 * half + 128], wd[...])
        for i in range(4):
            sgh[2 * i + half] = join(back[32 * i:32 * i + 16], back[32 * i + 16:32 * i + 32]).astype(BF16)
        scatter(sgh, rgh, half, GROUPS["zgh"])

    def reduce_and_share(parts, whole, base, share_base):
        loop(1, 8, lambda i: arrived(parts.at[ring(i)], base + ring(i)))
        total = parts[0].astype(F32)
        for i in range(1, 8):
            total = total + parts[i].astype(F32)
        whole[my_q] = total.astype(BF16)

        def one(i):
            to = ring(i)
            copy(whole.at[my_q], whole.at[my_q], share_base + to, share_base + r, (dp, to, c)).start()
        loop(1, 8, one)

    def gathered(whole, share_base):
        def one(i):
            of = ring(i)
            arrived(whole.at[of // 2 + 4 * lax.rem(of, 2)], share_base + of)
        loop(1, 8, one)

    reduce_and_share(rgu, agu, GROUPS["zgu"], GROUPS["agu"])
    reduce_and_share(rgh, agh, GROUPS["zgh"], GROUPS["agh"])

    def to_sibling(kept, given, name):
        def one(q):
            kept[q] = part_f[pl.ds(pl.multiple_of(32 * q + 16 * (1 - k), 16), 16), :].astype(BF16)
        loop(0, 8, one)
        copy(kept, given, GROUPS[name], GROUPS[name], sib).start()

    def to_owners(given, folded, landed, name, base):
        arrived(given, GROUPS[name])

        def one(q):
            tile = part_f[pl.ds(pl.multiple_of(32 * q + 16 * k, 16), 16), :] + given[q].astype(F32)
            for dx in range(2):
                folded[2 * q + dx] = fold(tile[8 * dx:8 * dx + 8]).astype(BF16)
                to, slot = chip(2 * q + dx)

                @pl.when(2 * q + dx > 0)
                def _():
                    copy(folded.at[2 * q + dx], landed.at[slot], base + 2 * q + dx, base + slot, to).start()
        loop(0, 8, one)
        landed[0] = folded[0]

    def finish(landed, out, base):
        loop(1, 16, lambda j: arrived(landed.at[j], base + j))
        total = landed[0].astype(F32)
        for j in range(1, 16):
            total = total + landed[j].astype(F32)
        out[...] = jnp.concatenate([total[:8], total[8:]], axis=1).astype(out.dtype)

    gathered(agu, GROUPS["agu"])
    copy(agu, pu, GROUPS["pu"], GROUPS["pu"], peer).start()

    def forward(q):
        gate, up = part(agu[q].astype(F32))
        hidden = gate * jax.nn.sigmoid(gate) * up
        hid[pl.ds(pl.multiple_of(32 * q, 32), 32), :] = hidden[:, :448].astype(BF16)
    loop(0, 8, forward)
    part_f[...] = dot(hid[...], wd[...])
    to_sibling(lo_s, lo_i, "lo_sib")
    to_owners(lo_i, lo_t, lo_r, "lo_sib", GROUPS["lo"])

    def backward(joined, halves, first):
        def one(q):
            gate, up = part(joined[q].astype(F32))
            grad = jnp.concatenate(part(halves[q].astype(F32)), axis=0)
            sig = jax.nn.sigmoid(gate)
            at = pl.ds(pl.multiple_of(first + 32 * q, 32), 32)
            gg[at, :] = (grad * up * sig * (1.0 + gate * (1.0 - sig)))[:, :448].astype(BF16)
            gu[at, :] = (grad * (gate * sig))[:, :448].astype(BF16)
        loop(0, 8, one)

    gathered(agh, GROUPS["agh"])
    copy(agh, ph, GROUPS["ph"], GROUPS["ph"], peer).start()
    backward(agu, agh, 0)
    part_f[...] = dot_nt(gg[:256], wg[...]) + dot_nt(gu[:256], wu[...])
    to_sibling(gi_s, gi_i, "gi_sib")
    to_owners(gi_i, gi_t, gi_r, "gi_sib", GROUPS["gi"])
    finish(lo_r, lo_out, GROUPS["lo"])

    arrived(px, GROUPS["px"])
    arrived(pu, GROUPS["pu"])
    arrived(ph, GROUPS["ph"])
    backward(pu, ph, 256)

    def weights(i):
        at = pl.ds(pl.multiple_of(256 * i, 256), 256)
        for grad, out in ((gg, gg_out), (gu, gu_out)):
            out[at, :] = (dot_tn(x[:, at], grad[:256]) + dot_tn(px[:, at], grad[256:])).astype(BF16)
    loop(0, 4, weights)
    finish(gi_r, gi_out, GROUPS["gi"])

    def drain(j):
        left(gx.at[k, 0], GROUPS["tok"] + j)
        left(gc.at[k, 0], GROUPS["cot"] + j)
        left(lo_t.at[j], GROUPS["lo"] + j)
        left(gi_t.at[j], GROUPS["gi"] + j)
    loop(1, 16, drain)

    def drain_row(i):
        to = ring(i)
        left(sgu.at[to], GROUPS["zgu"] + to)
        left(sgh.at[to], GROUPS["zgh"] + to)
        left(agu.at[my_q], GROUPS["agu"] + to)
        left(agh.at[my_q], GROUPS["agh"] + to)
    loop(1, 8, drain_row)
    for half in range(2):
        left(gx.at[k, pl.ds(8 * half, 8)], GROUPS["tok_sib"] + half)
        left(gc.at[k, pl.ds(8 * half, 8)], GROUPS["cot_sib"] + half)
    left(x, GROUPS["px"])
    left(agu, GROUPS["pu"])
    left(agh, GROUPS["ph"])
    left(lo_s, GROUPS["lo_sib"])
    left(gi_s, GROUPS["gi_sib"])


def body(tokens, gate_weight, up_weight, down_weight, cotangent):
    vmem = pl.BlockSpec(memory_space=pltpu.VMEM)
    anywhere = pl.BlockSpec(memory_space=pl.ANY)
    scratch = [
        ((1024, 448), BF16), ((1024, 448), BF16), ((448, 1024), BF16),
        ((2, 16, 16, 512), BF16), ((2, 16, 16, 512), BF16),
        ((256, 1024), BF16), ((256, 1024), BF16), ((256, 1024), BF16),
        ((8, 32, 896), BF16), ((8, 32, 896), BF16), ((8, 16, 896), BF16), ((8, 16, 896), BF16),
        ((8, 32, 896), BF16), ((8, 16, 896), BF16), ((8, 32, 896), BF16), ((8, 16, 896), BF16),
        ((256, 448), BF16), ((512, 448), BF16), ((512, 448), BF16),
        ((256, 1024), F32),
        ((8, 16, 1024), BF16), ((8, 16, 1024), BF16), ((8, 16, 1024), BF16), ((8, 16, 1024), BF16),
        ((16, 16, 512), BF16), ((16, 16, 512), BF16), ((16, 16, 512), BF16), ((16, 16, 512), BF16),
    ]
    return pl.pallas_call(
        kernel,
        out_shape=(
            jax.ShapeDtypeStruct((8, 1024), BF16),
            jax.ShapeDtypeStruct((8, 1024), BF16),
            jax.ShapeDtypeStruct((1024, 448), BF16),
            jax.ShapeDtypeStruct((1024, 448), BF16),
        ),
        in_specs=[vmem, anywhere, anywhere, anywhere, vmem],
        out_specs=(vmem, vmem, vmem, vmem),
        scratch_shapes=[pltpu.VMEM(shape, kind) for shape, kind in scratch]
        + [pltpu.SemaphoreType.DMA((N_SEM,)), pltpu.SemaphoreType.DMA((N_SEM,)), pltpu.SemaphoreType.DMA((3,))],
        compiler_params=pltpu.CompilerParams(
            collective_id=0, has_side_effects=True, vmem_limit_bytes=48 * 1024 * 1024
        ),
        cost_estimate=pl.CostEstimate(flops=2400000000, bytes_accessed=5000000, transcendentals=250000),
        name="swiglu_block",
    )(tokens, gate_weight, up_weight, down_weight, cotangent)


def solution(mesh):
    return jax.shard_map(
        body,
        mesh=mesh,
        in_specs=(
            P(("dp", "col"), "row"),
            P("row", "col"),
            P("row", "col"),
            P("col", "row"),
            P(("dp", "col"), "row"),
        ),
        out_specs=(
            P(("dp", "col"), "row"),
            P(("dp", "col"), "row"),
            P("row", "col"),
            P("row", "col"),
        ),
        check_vma=False,
    )
```

time: 500 us -> 90.4 us (0.18)
  the two profiles are of different devices: /device:TPU:1 before, /device:TPU:21 now
where the time goes in v1:
time: 90.4 us; the launch traced here: 90.2 us
  Pallas kernels  80.5 us (89%)
  local copies, waits for them, and re-layouts  9 us (10%)
    pallas_call x1, Pallas kernels, body(): pl.pallas_call(kernel, out_shape=(jax.ShapeDtypeStruct((8, 1024), BF16),...  80.5 us
    unnamed x14, local copies, waits for them, and re-layouts  6.48 us
    pallas_call x2, local copies, waits for them, and re-layouts, body(): pl.pallas_call(kernel, out_shape=(jax.ShapeDtypeStruct((8, 1024), BF16),...  2.52 us

profile of v1, /device:TPU:21, one launch (start us, length us, event | category | flops | bytes accessed | tf_op | source)
XLA Modules:
  0.0 90.2 jit_solution(18360966830371990334)
XLA Ops:
  0.6 0.0 copy-start.4
  0.6 1.5 %copy.9.wg_hbm = bf16[1024,448]{1,0:T(8,128)(2,1)S(1)} copy(bf16[1024,448]{0,1:T(8,128)(2,1)} %param.6) | data formatting | bytes 1835008 | tf_op args[1]
  2.2 0.0 copy-done.4
  2.2 0.0 copy-start.2
  2.2 0.0 copy-start.3
  2.2 1.3 %copy.10.wu_hbm = bf16[1024,448]{1,0:T(8,128)(2,1)} copy(bf16[1024,448]{0,1:T(8,128)(2,1)S(1)} %copy-done.4) | data formatting | bytes 1835008 | tf_op args[2]
  3.5 0.0 copy-done.2
  3.5 0.0 copy-done.3
  3.5 0.0 copy-start
  3.5 1.2 %copy-done = bf16[1024,448]{1,0:T(8,128)(2,1)S(1)} copy-done((bf16[1024,448]{1,0:T(8,128)(2,1)S(1)}, bf16[1024,448]{1,0:T(8,128)(2,1)}, u32[]{:S(2)}) %copy-start) | copy-done | bytes 917528
  4.8 0.0 copy-start.1
  4.8 1.2 %copy-done.1 = bf16[448,1024]{1,0:T(8,128)(2,1)S(1)} copy-done((bf16[448,1024]{1,0:T(8,128)(2,1)S(1)}, bf16[448,1024]{1,0:T(8,128)(2,1)}, u32[]{:S(2)}) %copy-start.1) | copy-done | bytes 917528
  5.9 80.5 %swiglu_block.1 = (bf16[8,1024]{1,0:T(8,128)(2,1)S(1)}, bf16[8,1024]{1,0:T(8,128)(2,1)S(1)}, bf16[1024,448]{1,0:T(8,128)(2,1)S(1)}, bf16[1024,448]{1,0:T(8,128)(2,1)S(1)}) custom-call(bf16[8,1024]{1,0:T(8,128)(2,1)S(1)} %copy-done.2, bf16[1024,448]{1,0:T(8,128)(2,1)S(1)} %copy.9.wg_hbm, bf16[1024,448]{1,0:T(8,128)(2,1)S(1)} %copy-done, ...), custom_call_target="tpu_custom_call" | custom-call | flops 2400000000 | bytes 5000000 | tf_op jit(solution)/shard_map/swiglu_block/pallas_call | solution.py:304
  86.5 1.3 %copy.11 = bf16[1024,448]{0,1:T(8,128)(2,1)} copy(bf16[1024,448]{1,0:T(8,128)(2,1)S(1)} %get-tuple-element.6) | data formatting | bytes 1835008 | tf_op jit(solution)/shard_map/swiglu_block/pallas_call | solution.py:304
  87.7 1.3 %copy.12 = bf16[1024,448]{0,1:T(8,128)(2,1)} copy(bf16[1024,448]{1,0:T(8,128)(2,1)S(1)} %get-tuple-element.7) | data formatting | bytes 1835008 | tf_op jit(solution)/shard_map/swiglu_block/pallas_call | solution.py:304
  89.0 0.6 copy.15
  89.6 0.6 copy.16
Async XLA Ops:
  0.6 1.6 %copy-start.4 = (bf16[1024,448]{0,1:T(8,128)(2,1)S(1)}, bf16[1024,448]{0,1:T(8,128)(2,1)}, u32[]{:S(2)}) copy-start(bf16[1024,448]{0,1:T(8,128)(2,1)} %param.7) | copy-start | bytes 2752516
  2.2 1.3 %copy-start.2 = (bf16[8,1024]{1,0:T(8,128)(2,1)S(1)}, bf16[8,1024]{1,0:T(8,128)(2,1)}, u32[]{:S(2)}) copy-start(bf16[8,1024]{1,0:T(8,128)(2,1)} %tok_ref.1) | copy-start | bytes 49156
  2.2 1.3 %copy-start.3 = (bf16[8,1024]{1,0:T(8,128)(2,1)S(1)}, bf16[8,1024]{1,0:T(8,128)(2,1)}, u32[]{:S(2)}) copy-start(bf16[8,1024]{1,0:T(8,128)(2,1)} %cot_ref.1) | copy-start | bytes 49156
  3.5 1.2 %copy-start = (bf16[1024,448]{1,0:T(8,128)(2,1)S(1)}, bf16[1024,448]{1,0:T(8,128)(2,1)}, u32[]{:S(2)}) copy-start(bf16[1024,448]{1,0:T(8,128)(2,1)} %copy.10.wu_hbm) | copy-start | bytes 2752516
  4.8 1.2 %copy-start.1 = (bf16[448,1024]{1,0:T(8,128)(2,1)S(1)}, bf16[448,1024]{1,0:T(8,128)(2,1)}, u32[]{:S(2)}) copy-start(bf16[448,1024]{1,0:T(8,128)(2,1)} %wd_hbm.1) | copy-start | bytes 2752516

commit v2 on v1

v2 whole, which is shorter than its diff:
```python
import functools

import jax
import jax.numpy as jnp
from jax import lax
from jax.experimental import pallas as pl
from jax.experimental.pallas import tpu as pltpu
from jax.sharding import PartitionSpec as P

MESH = pl.DeviceIdType.MESH
F32, BF16 = jnp.float32, jnp.bfloat16

GROUPS = {}
N_SEM = 0
for _name, _count in (
    ("tok", 16), ("cot", 16), ("tok_sib", 2), ("cot_sib", 2), ("zgu", 8), ("zgh", 8), ("agu", 8), ("agh", 8),
    ("px", 1), ("px_sib", 1), ("pg", 8), ("lo_sib", 2), ("gi_sib", 2), ("lo", 16), ("gi", 16),
):
    GROUPS[_name] = N_SEM
    N_SEM += _count


def dot(a, b):
    return lax.dot_general(a, b, (((1,), (0,)), ((), ())), preferred_element_type=F32)


def dot_nt(a, b):
    return lax.dot_general(a, b, (((1,), (1,)), ((), ())), preferred_element_type=F32)


def dot_tn(a, b):
    return lax.dot_general(a, b, (((0,), (0,)), ((), ())), preferred_element_type=F32)


def join(a, b):
    return jnp.concatenate([a[:, :384], b[:, :384], a[:, 384:448], b[:, 384:448]], axis=1)


def part(x):
    tail = x[:, 768:896]
    return (
        jnp.concatenate([x[:, :384], tail], axis=1),
        jnp.concatenate([x[:, 384:768], pltpu.roll(tail, 64, 1)], axis=1),
    )


def fold(x):
    return jnp.concatenate([x[:, :512], x[:, 512:]], axis=0)


def kernel(
    tok_ref, wg_hbm, wu_hbm, wd_hbm, cot_ref,
    x_out, g_out, lo_out, gi_out,
    wj, wd, gx, gc, gp, x, cx, sgu, rgu, lgu, cgu, sgh, rgh, lgh, cgh, agu, agh,
    hid, gl, g, lo_f, gi_f, lo_s, lo_i, gi_s, gi_i, lo_t, lo_r, gi_t, gi_r,
    send, recv, wsem,
):
    dp, r, c = lax.axis_index("dp"), lax.axis_index("row"), lax.axis_index("col")
    k = lax.rem(c, 2)
    xh = lax.rem(c // 2, 2)
    y = c // 4
    odd_row = lax.rem(r, 2)
    sib = (dp, r, c + 1 - 2 * k)
    peer = (1 - dp, r, c)

    def chip(j):
        q, dx = j // 2, lax.rem(j, 2)
        odd = lax.rem(q, 2)
        dy = odd * ((q + 1) // 2) + (1 - odd) * (8 - q // 2)
        back = jnp.where(q == 0, 0, jnp.where(q == 7, 7, q - 1 + 2 * odd))
        to = (lax.rem(y + dy, 8) * 2 + lax.rem(xh + dx, 2)) * 2 + k
        return (dp, r, to), back * 2 + dx

    def at_row(offset):
        return lax.rem(r + offset + 8, 8)

    def row_device(offset):
        return (dp, at_row(offset), c)

    def group_of(row):
        return row // 2 + 4 * lax.rem(row, 2)

    def ring(i):
        odd = lax.rem(i, 2)
        return lax.rem(r + odd * ((i + 1) // 2) + (1 - odd) * (8 - i // 2), 8)

    def copy(src, dst, s, d, to):
        return pltpu.make_async_remote_copy(
            src_ref=src, dst_ref=dst, send_sem=send.at[s], recv_sem=recv.at[d], device_id=to, device_id_type=MESH
        )

    def arrived(dst, d):
        pltpu.make_async_copy(dst, dst, recv.at[d]).wait()

    def left(src, s):
        pltpu.make_async_copy(src, src, send.at[s]).wait()

    def loop(lo, hi, body):
        def step(i, carry):
            body(i)
            return carry
        lax.fori_loop(lo, hi, step, 0)

    def rows(start, count):
        return pl.ds(pl.multiple_of(start, count), count)

    loads = [
        pltpu.make_async_copy(a, b, wsem.at[i])
        for i, (a, b) in enumerate((
            (wg_hbm.at[:384], wj.at[:384]),
            (wu_hbm.at[:384], wj.at[384:768]),
            (wg_hbm.at[384:], wj.at[768:832]),
            (wu_hbm.at[384:], wj.at[832:]),
            (wd_hbm, wd),
        ))
    ]
    for load in loads:
        load.start()

    barrier = pltpu.get_barrier_semaphore()

    def greet(to):
        pl.semaphore_signal(barrier, inc=1, device_id=to, device_id_type=MESH)

    loop(1, 16, lambda j: greet(chip(j)[0]))
    loop(1, 5, lambda i: greet((dp, ring(i), c)))
    greet(sib)
    greet(peer)
    gx[k, 0] = fold(tok_ref[...].astype(F32)).astype(BF16)
    gc[k, 0] = fold(cot_ref[...].astype(F32)).astype(BF16)
    pl.semaphore_wait(barrier, 21)

    def spread(buf, base):
        def one(j):
            to, slot = chip(j)
            copy(buf.at[k, 0], buf.at[k, slot], base + j, base + slot, to).start()
        loop(1, 16, one)

    spread(gx, GROUPS["tok"])
    spread(gc, GROUPS["cot"])

    def unfold(buf, into, first, q):
        for core in range(2):
            a, b = buf[core, 2 * q].astype(F32), buf[core, 2 * q + 1].astype(F32)
            at = rows(first + 32 * q + 16 * core, 16)
            into[at, :512] = jnp.concatenate([a[:8], b[:8]], axis=0).astype(BF16)
            into[at, 512:] = jnp.concatenate([a[8:], b[8:]], axis=0).astype(BF16)

    def collect(buf, into, half, base, sib_base):
        lo = 8 * half
        loop(max(lo, 1), lo + 8, lambda j: arrived(buf.at[k, j], base + j))
        mine = buf.at[k, pl.ds(lo, 8)]
        copy(mine, mine, sib_base + half, sib_base + half, sib).start()
        arrived(buf.at[1 - k, pl.ds(lo, 8)], sib_base + half)
        loop(4 * half, 4 * half + 4, lambda q: unfold(buf, into, 0, q))

    def scatter(src, near, far, half, base):
        @pl.when(odd_row == half)
        def _():
            copy(src.at[at_row(4)], far.at[2], base + 6, base + 6, row_device(2 + 4 * odd_row)).start()

        @pl.when(odd_row != half)
        def _():
            copy(src.at[at_row(3)], far.at[0], base + 4, base + 4, row_device(1)).start()
            copy(src.at[at_row(-3)], far.at[1], base + 5, base + 5, row_device(-1)).start()
            copy(src.at[at_row(1)], near.at[0], base, base, row_device(1)).start()
            copy(src.at[at_row(-1)], near.at[1], base + 1, base + 1, row_device(-1)).start()

    def relay(src, near, far, both, base, parity):
        @pl.when(odd_row == parity)
        def _():
            for i in range(3):
                arrived(far.at[i], base + 4 + i)
            third = far[2].astype(F32)
            up_sum = src[at_row(2)].astype(F32) + far[0].astype(F32)
            down_sum = src[at_row(-2)].astype(F32) + far[1].astype(F32)
            if parity == 0:
                up_sum = up_sum + third
            else:
                down_sum = down_sum + third
            both[0] = up_sum.astype(BF16)
            both[1] = down_sum.astype(BF16)
            copy(both.at[0], near.at[2], base + 2, base + 2, row_device(2)).start()
            copy(both.at[1], near.at[3], base + 3, base + 3, row_device(-2)).start()

    def reduce_and_share(src, near, whole, base, share):
        for i in range(4):
            arrived(near.at[i], base + i)
        total = src[r].astype(F32)
        for i in range(4):
            total = total + near[i].astype(F32)
        own = group_of(r)
        whole[own] = total.astype(BF16)
        block = whole.at[own]
        copy(block, block, share + 3, share + 4, row_device(2)).start()
        copy(block, block, share + 4, share + 3, row_device(-2)).start()
        copy(block, block, share + 1, share + 2, row_device(1)).start()
        copy(block, block, share + 2, share + 1, row_device(-1)).start()

    def pass_on(whole, share):
        above, below = whole.at[group_of(at_row(2))], whole.at[group_of(at_row(-2))]
        arrived(above, share + 3)
        arrived(below, share + 4)
        copy(below, below, share + 5, share + 6, row_device(1)).start()
        copy(above, above, share + 6, share + 5, row_device(-1)).start()
        last = whole.at[group_of(at_row(6 + 4 * odd_row))]
        copy(last, last, share + 7, share + 7, row_device(2 + 4 * odd_row)).start()

    def come(whole, share, lo, hi):
        loop(lo, hi, lambda i: arrived(whole.at[group_of(ring(i))], share + i))

    for half in range(2):
        collect(gx, x, half, GROUPS["tok"], GROUPS["tok_sib"])
        if half == 0:
            for load in loads[:4]:
                load.wait()
        pre = dot_nt(x[128 * half:128 * half + 128], wj[...])
        for i in range(4):
            sgu[2 * i + half] = pre[32 * i:32 * i + 32].astype(BF16)
        scatter(sgu, rgu, lgu, half, GROUPS["zgu"])
    copy(gx.at[k], gp.at[k], GROUPS["px"], GROUPS["px"], peer).start()
    relay(sgu, rgu, lgu, cgu, GROUPS["zgu"], 0)
    for half in range(2):
        collect(gc, cx, half, GROUPS["cot"], GROUPS["cot_sib"])
        if half == 0:
            loads[4].wait()
        back = dot_nt(cx[128 * half:128 * half + 128], wd[...])
        for i in range(4):
            sgh[2 * i + half] = join(back[32 * i:32 * i + 16], back[32 * i + 16:32 * i + 32]).astype(BF16)
        scatter(sgh, rgh, lgh, half, GROUPS["zgh"])
        if half == 0:
            relay(sgu, rgu, lgu, cgu, GROUPS["zgu"], 1)
    relay(sgh, rgh, lgh, cgh, GROUPS["zgh"], 0)
    reduce_and_share(sgu, rgu, agu, GROUPS["zgu"], GROUPS["agu"])
    relay(sgh, rgh, lgh, cgh, GROUPS["zgh"], 1)
    reduce_and_share(sgh, rgh, agh, GROUPS["zgh"], GROUPS["agh"])
    arrived(gp.at[k], GROUPS["px"])
    copy(gp.at[k], gp.at[k], GROUPS["px_sib"], GROUPS["px_sib"], sib).start()

    def to_sibling(sums, kept, given, turn, name):
        def one(i):
            kept[i] = sums[rows(32 * i + 16 * (1 - k), 16), :].astype(BF16)
        loop(4 * turn, 4 * turn + 4, one)
        some = pl.ds(4 * turn, 4)
        copy(kept.at[some], given.at[some], GROUPS[name] + turn, GROUPS[name] + turn, sib).start()

    def to_owners(sums, given, folded, landed, turn, name, base):
        arrived(given.at[pl.ds(4 * turn, 4)], GROUPS[name] + turn)

        def one(i):
            tile = sums[rows(32 * i + 16 * k, 16), :] + given[i].astype(F32)
            q = group_of(ring(i))
            for dx in range(2):
                j = 2 * q + dx
                block = fold(tile[8 * dx:8 * dx + 8]).astype(BF16)

                @pl.when(j == 0)
                def _():
                    landed[0] = block

                @pl.when(j > 0)
                def _():
                    folded[j] = block
                    to, slot = chip(j)
                    copy(folded.at[j], landed.at[slot], base + j, base + slot, to).start()
        loop(4 * turn, 4 * turn + 4, one)

    def forward(turn):
        def one(i):
            gate, up = part(agu[group_of(ring(i))].astype(F32))
            hidden = gate * jax.nn.sigmoid(gate) * up
            hid[rows(32 * i, 32), :] = hidden[:, :448].astype(BF16)
        loop(4 * turn, 4 * turn + 4, one)
        lines = slice(128 * turn, 128 * turn + 128)
        lo_f[lines] = dot(hid[lines], wd[...])
        to_sibling(lo_f, lo_s, lo_i, turn, "lo_sib")

    def backward(turn):
        def one(i):
            q = group_of(ring(i))
            gate, up = part(agu[q].astype(F32))
            grad = jnp.concatenate(part(agh[q].astype(F32)), axis=0)
            sig = jax.nn.sigmoid(gate)
            both = join(grad * up * sig * (1.0 + gate * (1.0 - sig)), grad * (gate * sig)).astype(BF16)
            gl[rows(32 * i, 32), :] = both
            g[rows(32 * q, 32), :] = both
            copy(
                g.at[rows(32 * q, 32)], g.at[rows(256 + 32 * q, 32)], GROUPS["pg"] + q, GROUPS["pg"] + q, peer
            ).start()
        loop(4 * turn, 4 * turn + 4, one)
        lines = slice(128 * turn, 128 * turn + 128)
        gi_f[lines] = dot(gl[lines], wj[...])
        to_sibling(gi_f, gi_s, gi_i, turn, "gi_sib")

    pass_on(agu, GROUPS["agu"])
    come(agu, GROUPS["agu"], 1, 3)
    forward(0)
    pass_on(agh, GROUPS["agh"])
    come(agh, GROUPS["agh"], 1, 3)
    backward(0)
    to_owners(lo_f, lo_i, lo_t, lo_r, 0, "lo_sib", GROUPS["lo"])
    to_owners(gi_f, gi_i, gi_t, gi_r, 0, "gi_sib", GROUPS["gi"])
    come(agu, GROUPS["agu"], 5, 8)
    forward(1)
    come(agh, GROUPS["agh"], 5, 8)
    backward(1)
    to_owners(lo_f, lo_i, lo_t, lo_r, 1, "lo_sib", GROUPS["lo"])
    to_owners(gi_f, gi_i, gi_t, gi_r, 1, "gi_sib", GROUPS["gi"])

    arrived(gp.at[1 - k], GROUPS["px_sib"])
    loop(0, 8, lambda q: unfold(gp, x, 256, q))
    save_x = pltpu.make_async_copy(x, x_out, wsem.at[5])
    save_x.start()
    loop(1, 16, lambda j: arrived(lo_r.at[j], GROUPS["lo"] + j))
    save_lo = pltpu.make_async_copy(lo_r, lo_out, wsem.at[6])
    save_lo.start()
    loop(0, 8, lambda q: arrived(g.at[rows(256 + 32 * q, 32)], GROUPS["pg"] + q))
    save_g = pltpu.make_async_copy(g, g_out, wsem.at[7])
    save_g.start()
    loop(1, 16, lambda j: arrived(gi_r.at[j], GROUPS["gi"] + j))
    save_gi = pltpu.make_async_copy(gi_r, gi_out, wsem.at[8])
    save_gi.start()

    def drain(j):
        left(gx.at[k, 0], GROUPS["tok"] + j)
        left(gc.at[k, 0], GROUPS["cot"] + j)
        left(lo_t.at[j], GROUPS["lo"] + j)
        left(gi_t.at[j], GROUPS["gi"] + j)
    loop(1, 16, drain)

    def drain_row(i):
        left(sgu.at[0], GROUPS["zgu"] + i)
        left(sgh.at[0], GROUPS["zgh"] + i)
        left(agu.at[0], GROUPS["agu"] + i + 1)
        left(agh.at[0], GROUPS["agh"] + i + 1)
    loop(0, 7, drain_row)
    loop(0, 8, lambda q: left(g.at[rows(32 * q, 32)], GROUPS["pg"] + q))
    for half in range(2):
        left(gx.at[k, pl.ds(8 * half, 8)], GROUPS["tok_sib"] + half)
        left(gc.at[k, pl.ds(8 * half, 8)], GROUPS["cot_sib"] + half)
        left(lo_s.at[pl.ds(4 * half, 4)], GROUPS["lo_sib"] + half)
        left(gi_s.at[pl.ds(4 * half, 4)], GROUPS["gi_sib"] + half)
    left(gx.at[k], GROUPS["px"])
    left(gp.at[k], GROUPS["px_sib"])
    for save in (save_x, save_lo, save_g, save_gi):
        save.wait()


def finish(x_ref, g_ref, lo_ref, gi_ref, lo_out, gi_out, gg_out, gu_out):
    for parts, out in ((lo_ref, lo_out), (gi_ref, gi_out)):
        total = parts[0].astype(F32)
        for j in range(1, 16):
            total = total + parts[j].astype(F32)
        out[...] = jnp.concatenate([total[:8], total[8:]], axis=1).astype(BF16)
    grads = dot_tn(g_ref[...], x_ref[...]).astype(BF16)
    gg_out[:384] = grads[:384]
    gu_out[:384] = grads[384:768]
    gg_out[384:] = grads[768:832]
    gu_out[384:] = grads[832:]


def body(tokens, gate_weight, up_weight, down_weight, cotangent):
    vmem = pl.BlockSpec(memory_space=pltpu.VMEM)
    anywhere = pl.BlockSpec(memory_space=pl.ANY)
    scratch = [
        ((896, 1024), BF16), ((448, 1024), BF16),
        ((2, 16, 16, 512), BF16), ((2, 16, 16, 512), BF16), ((2, 16, 16, 512), BF16),
        ((512, 1024), BF16), ((256, 1024), BF16),
        ((8, 32, 896), BF16), ((4, 32, 896), BF16), ((3, 32, 896), BF16), ((2, 32, 896), BF16),
        ((8, 16, 896), BF16), ((4, 16, 896), BF16), ((3, 16, 896), BF16), ((2, 16, 896), BF16),
        ((8, 32, 896), BF16), ((8, 16, 896), BF16),
        ((256, 448), BF16), ((256, 896), BF16), ((512, 896), BF16),
        ((256, 1024), F32), ((256, 1024), F32),
        ((8, 16, 1024), BF16), ((8, 16, 1024), BF16), ((8, 16, 1024), BF16), ((8, 16, 1024), BF16),
        ((16, 16, 512), BF16), ((16, 16, 512), BF16), ((16, 16, 512), BF16), ((16, 16, 512), BF16),
    ]
    grant = 61 * 1024 * 1024
    x, g, lo, gi = pl.pallas_call(
        kernel,
        out_shape=(
            jax.ShapeDtypeStruct((512, 1024), BF16),
            jax.ShapeDtypeStruct((512, 896), BF16),
            jax.ShapeDtypeStruct((16, 16, 512), BF16),
            jax.ShapeDtypeStruct((16, 16, 512), BF16),
        ),
        in_specs=[vmem, anywhere, anywhere, anywhere, vmem],
        out_specs=(anywhere,) * 4,
        scratch_shapes=[pltpu.VMEM(shape, kind) for shape, kind in scratch]
        + [pltpu.SemaphoreType.DMA((N_SEM,)), pltpu.SemaphoreType.DMA((N_SEM,)), pltpu.SemaphoreType.DMA((9,))],
        compiler_params=pltpu.CompilerParams(collective_id=0, has_side_effects=True, vmem_limit_bytes=grant),
        cost_estimate=pl.CostEstimate(flops=1500000000, bytes_accessed=5000000, transcendentals=250000),
        name="swiglu_block",
    )(tokens, gate_weight.T, up_weight.T, down_weight, cotangent)
    layer_output, grad_input, grad_gate, grad_up = pl.pallas_call(
        finish,
        out_shape=(
            jax.ShapeDtypeStruct((8, 1024), BF16),
            jax.ShapeDtypeStruct((8, 1024), BF16),
            jax.ShapeDtypeStruct((448, 1024), BF16),
            jax.ShapeDtypeStruct((448, 1024), BF16),
        ),
        in_specs=[vmem] * 4,
        out_specs=(vmem,) * 4,
        compiler_params=pltpu.CompilerParams(vmem_limit_bytes=grant),
        cost_estimate=pl.CostEstimate(flops=940000000, bytes_accessed=4500000, transcendentals=0),
        name="finish",
    )(x, g, lo, gi)
    return layer_output, grad_input, grad_gate.T, grad_up.T


def solution(mesh):
    return jax.shard_map(
        body,
        mesh=mesh,
        in_specs=(
            P(("dp", "col"), "row"),
            P("row", "col"),
            P("row", "col"),
            P("col", "row"),
            P(("dp", "col"), "row"),
        ),
        out_specs=(
            P(("dp", "col"), "row"),
            P(("dp", "col"), "row"),
            P("row", "col"),
            P("row", "col"),
        ),
        check_vma=False,
    )
```

time: 90.4 us -> 74.4 us (0.82)
  the two profiles are of different devices: /device:TPU:21 before, /device:TPU:1 now
where the time goes in v2:
time: 74.4 us; the launch traced here: 74 us
  Pallas kernels  73.4 us (99%)
    pallas_call x1, Pallas kernels, body(): pl.pallas_call(kernel, out_shape=(jax.ShapeDtypeStruct((512, 1024), BF16)...  69.4 us
    pallas_call x1, Pallas kernels, body(): pl.pallas_call(finish, out_shape=(jax.ShapeDtypeStruct((8, 1024), BF16),...  3.98 us

profile of v2, /device:TPU:1, one launch (start us, length us, event | category | flops | bytes accessed | tf_op | source)
XLA Modules:
  0.0 74.0 jit_solution(9859972025129748730)
XLA Ops:
  0.6 69.4 %swiglu_block.1 = (bf16[512,1024]{1,0:T(8,128)(2,1)}, bf16[512,896]{1,0:T(8,128)(2,1)}, bf16[16,16,512]{2,1,0:T(8,128)(2,1)}, bf16[16,16,512]{2,1,0:T(8,128)(2,1)}) custom-call(bf16[8,1024]{1,0:T(8,128)(2,1)} %tok_ref.1, bf16[448,1024]{1,0:T(8,128)(2,1)} %bitcast.4, bf16[448,1024]{1,0:T(8,128)(2,1)} %bitcast.5, bf16[448,1024]{1,0:T(8,128)(2,1)} %wd_hbm.1, ...), custom_call_target="tpu_custom_call" | custom-call | flops 1500000000 | bytes 5000000 | tf_op jit(solution)/shard_map/swiglu_block/pallas_call | solution.py:378
  70.1 4.0 %finish.1 = (bf16[8,1024]{1,0:T(8,128)(2,1)}, bf16[8,1024]{1,0:T(8,128)(2,1)}, bf16[448,1024]{1,0:T(8,128)(2,1)}, bf16[448,1024]{1,0:T(8,128)(2,1)}) custom-call(bf16[512,1024]{1,0:T(8,128)(2,1)} %get-tuple-element.12.x_ref, bf16[512,896]{1,0:T(8,128)(2,1)} %get-tuple-element.13.g_ref, bf16[16,16,512]{2,1,0:T(8,128)(2,1)} %get-tuple-element.14.lo_ref, ...), custom_call_target="tpu_custom_call" | custom-call | flops 940000000 | bytes 4500000 | tf_op jit(solution)/shard_map/finish/pallas_call | solution.py:394

commit v3 on v2

--- a/solution.py
+++ b/solution.py
@@ -132,8 +132,8 @@
 
     def spread(buf, base):
         def one(j):
-            to, slot = chip(j)
-            copy(buf.at[k, 0], buf.at[k, slot], base + j, base + slot, to).start()
+            to, slot = chip(16 - j)
+            copy(buf.at[k, 0], buf.at[k, slot], base + 16 - j, base + slot, to).start()
         loop(1, 16, one)
 
     spread(gx, GROUPS["tok"])
@@ -146,12 +146,15 @@
             into[at, :512] = jnp.concatenate([a[:8], b[:8]], axis=0).astype(BF16)
             into[at, 512:] = jnp.concatenate([a[8:], b[8:]], axis=0).astype(BF16)
 
-    def collect(buf, into, half, base, sib_base):
-        lo = 8 * half
-        loop(max(lo, 1), lo + 8, lambda j: arrived(buf.at[k, j], base + j))
-        mine = buf.at[k, pl.ds(lo, 8)]
-        copy(mine, mine, sib_base + half, sib_base + half, sib).start()
-        arrived(buf.at[1 - k, pl.ds(lo, 8)], sib_base + half)
+    def pair_up(buf, base, sib_base):
+        for half in (1, 0):
+            lo = 8 * half
+            loop(max(lo, 1), lo + 8, lambda j: arrived(buf.at[k, j], base + j))
+            mine = buf.at[k, pl.ds(lo, 8)]
+            copy(mine, mine, sib_base + half, sib_base + half, sib).start()
+
+    def collect(buf, into, half, sib_base):
+        arrived(buf.at[1 - k, pl.ds(8 * half, 8)], sib_base + half)
         loop(4 * half, 4 * half + 4, lambda q: unfold(buf, into, 0, q))
 
     def scatter(src, near, far, half, base):
@@ -209,9 +212,10 @@
     def come(whole, share, lo, hi):
         loop(lo, hi, lambda i: arrived(whole.at[group_of(ring(i))], share + i))
 
-    for half in range(2):
-        collect(gx, x, half, GROUPS["tok"], GROUPS["tok_sib"])
-        if half == 0:
+    pair_up(gx, GROUPS["tok"], GROUPS["tok_sib"])
+    for half in (1, 0):
+        collect(gx, x, half, GROUPS["tok_sib"])
+        if half == 1:
             for load in loads[:4]:
                 load.wait()
         pre = dot_nt(x[128 * half:128 * half + 128], wj[...])
@@ -219,59 +223,69 @@
             sgu[2 * i + half] = pre[32 * i:32 * i + 32].astype(BF16)
         scatter(sgu, rgu, lgu, half, GROUPS["zgu"])
     copy(gx.at[k], gp.at[k], GROUPS["px"], GROUPS["px"], peer).start()
+    relay(sgu, rgu, lgu, cgu, GROUPS["zgu"], 1)
     relay(sgu, rgu, lgu, cgu, GROUPS["zgu"], 0)
-    for half in range(2):
-        collect(gc, cx, half, GROUPS["cot"], GROUPS["cot_sib"])
-        if half == 0:
+    pair_up(gc, GROUPS["cot"], GROUPS["cot_sib"])
+    for half in (1, 0):
+        collect(gc, cx, half, GROUPS["cot_sib"])
+        if half == 1:
             loads[4].wait()
         back = dot_nt(cx[128 * half:128 * half + 128], wd[...])
         for i in range(4):
             sgh[2 * i + half] = join(back[32 * i:32 * i + 16], back[32 * i + 16:32 * i + 32]).astype(BF16)
         scatter(sgh, rgh, lgh, half, GROUPS["zgh"])
-        if half == 0:
-            relay(sgu, rgu, lgu, cgu, GROUPS["zgu"], 1)
+    relay(sgh, rgh, lgh, cgh, GROUPS["zgh"], 1)
     relay(sgh, rgh, lgh, cgh, GROUPS["zgh"], 0)
     reduce_and_share(sgu, rgu, agu, GROUPS["zgu"], GROUPS["agu"])
-    relay(sgh, rgh, lgh, cgh, GROUPS["zgh"], 1)
     reduce_and_share(sgh, rgh, agh, GROUPS["zgh"], GROUPS["agh"])
     arrived(gp.at[k], GROUPS["px"])
     copy(gp.at[k], gp.at[k], GROUPS["px_sib"], GROUPS["px_sib"], sib).start()
 
+    first, last = (0, 5), (5, 8)
+
     def to_sibling(sums, kept, given, turn, name):
         def one(i):
             kept[i] = sums[rows(32 * i + 16 * (1 - k), 16), :].astype(BF16)
-        loop(4 * turn, 4 * turn + 4, one)
-        some = pl.ds(4 * turn, 4)
+        lo, hi = (first, last)[turn]
+        loop(lo, hi, one)
+        some = pl.ds(lo, hi - lo)
         copy(kept.at[some], given.at[some], GROUPS[name] + turn, GROUPS[name] + turn, sib).start()
 
     def to_owners(sums, given, folded, landed, turn, name, base):
-        arrived(given.at[pl.ds(4 * turn, 4)], GROUPS[name] + turn)
-
-        def one(i):
-            tile = sums[rows(32 * i + 16 * k, 16), :] + given[i].astype(F32)
-            q = group_of(ring(i))
-            for dx in range(2):
-                j = 2 * q + dx
-                block = fold(tile[8 * dx:8 * dx + 8]).astype(BF16)
-
-                @pl.when(j == 0)
-                def _():
-                    landed[0] = block
-
-                @pl.when(j > 0)
-                def _():
-                    folded[j] = block
-                    to, slot = chip(j)
-                    copy(folded.at[j], landed.at[slot], base + j, base + slot, to).start()
-        loop(4 * turn, 4 * turn + 4, one)
+        lo, hi = (first, last)[turn]
+        arrived(given.at[pl.ds(lo, hi - lo)], GROUPS[name] + turn)
+
+        def one(step):
+            q = 7 - step
+            offset = lax.rem(2 * lax.rem(q, 4) + q // 4 - r + 8, 8)
+            i = jnp.where(offset == 0, 0, jnp.where(offset <= 4, 2 * offset - 1, 16 - 2 * offset))
+
+            @pl.when((i >= lo) & (i < hi))
+            def _():
+                tile = sums[rows(32 * i + 16 * k, 16), :] + given[i].astype(F32)
+                for dx in (1, 0):
+                    j = 2 * q + dx
+                    block = fold(tile[8 * dx:8 * dx + 8]).astype(BF16)
+
+                    @pl.when(j == 0)
+                    def _():
+                        landed[0] = block
+
+                    @pl.when(j > 0)
+                    def _():
+                        folded[j] = block
+                        to, slot = chip(j)
+                        copy(folded.at[j], landed.at[slot], base + j, base + slot, to).start()
+        loop(0, 8, one)
 
     def forward(turn):
         def one(i):
             gate, up = part(agu[group_of(ring(i))].astype(F32))
             hidden = gate * jax.nn.sigmoid(gate) * up
             hid[rows(32 * i, 32), :] = hidden[:, :448].astype(BF16)
-        loop(4 * turn, 4 * turn + 4, one)
-        lines = slice(128 * turn, 128 * turn + 128)
+        lo, hi = (first, last)[turn]
+        loop(lo, hi, one)
+        lines = slice(32 * lo, 32 * hi)
         lo_f[lines] = dot(hid[lines], wd[...])
         to_sibling(lo_f, lo_s, lo_i, turn, "lo_sib")
 
@@ -287,8 +301,9 @@
             copy(
                 g.at[rows(32 * q, 32)], g.at[rows(256 + 32 * q, 32)], GROUPS["pg"] + q, GROUPS["pg"] + q, peer
             ).start()
-        loop(4 * turn, 4 * turn + 4, one)
-        lines = slice(128 * turn, 128 * turn + 128)
+        lo, hi = (first, last)[turn]
+        loop(lo, hi, one)
+        lines = slice(32 * lo, 32 * hi)
         gi_f[lines] = dot(gl[lines], wj[...])
         to_sibling(gi_f, gi_s, gi_i, turn, "gi_sib")
 
@@ -302,9 +317,9 @@
     to_owners(gi_f, gi_i, gi_t, gi_r, 0, "gi_sib", GROUPS["gi"])
     come(agu, GROUPS["agu"], 5, 8)
     forward(1)
+    to_owners(lo_f, lo_i, lo_t, lo_r, 1, "lo_sib", GROUPS["lo"])
     come(agh, GROUPS["agh"], 5, 8)
     backward(1)
-    to_owners(lo_f, lo_i, lo_t, lo_r, 1, "lo_sib", GROUPS["lo"])
     to_owners(gi_f, gi_i, gi_t, gi_r, 1, "gi_sib", GROUPS["gi"])
 
     arrived(gp.at[1 - k], GROUPS["px_sib"])
@@ -338,8 +353,9 @@
     for half in range(2):
         left(gx.at[k, pl.ds(8 * half, 8)], GROUPS["tok_sib"] + half)
         left(gc.at[k, pl.ds(8 * half, 8)], GROUPS["cot_sib"] + half)
-        left(lo_s.at[pl.ds(4 * half, 4)], GROUPS["lo_sib"] + half)
-        left(gi_s.at[pl.ds(4 * half, 4)], GROUPS["gi_sib"] + half)
+        lo, hi = (first, last)[half]
+        left(lo_s.at[pl.ds(lo, hi - lo)], GROUPS["lo_sib"] + half)
+        left(gi_s.at[pl.ds(lo, hi - lo)], GROUPS["gi_sib"] + half)
     left(gx.at[k], GROUPS["px"])
     left(gp.at[k], GROUPS["px_sib"])
     for save in (save_x, save_lo, save_g, save_gi):

time: 74.4 us -> 71.6 us (0.962)
  Pallas kernels: 73.4 us -> 70.7 us
    pallas_call x1, Pallas kernels: 69.4 us -> 66.7 us  [body(): pl.pallas_call(kernel, out_shape=(jax.ShapeDtypeStruct((512, 1024), BF16)...]
where the time goes in v3:
time: 71.6 us; the launch traced here: 71.3 us
  Pallas kernels  70.7 us (99%)
    pallas_call x1, Pallas kernels, body(): pl.pallas_call(kernel, out_shape=(jax.ShapeDtypeStruct((512, 1024), BF16)...  66.7 us
    pallas_call x1, Pallas kernels, body(): pl.pallas_call(finish, out_shape=(jax.ShapeDtypeStruct((8, 1024), BF16),...  3.98 us

profile of v3, /device:TPU:1, one launch (start us, length us, event | category | flops | bytes accessed | tf_op | source)
XLA Modules:
  0.0 71.3 jit_solution(1218204228242478821)
XLA Ops:
  0.6 66.7 %swiglu_block.1 = (bf16[512,1024]{1,0:T(8,128)(2,1)}, bf16[512,896]{1,0:T(8,128)(2,1)}, bf16[16,16,512]{2,1,0:T(8,128)(2,1)}, bf16[16,16,512]{2,1,0:T(8,128)(2,1)}) custom-call(bf16[8,1024]{1,0:T(8,128)(2,1)} %tok_ref.1, bf16[448,1024]{1,0:T(8,128)(2,1)} %bitcast.4, bf16[448,1024]{1,0:T(8,128)(2,1)} %bitcast.5, bf16[448,1024]{1,0:T(8,128)(2,1)} %wd_hbm.1, ...), custom_call_target="tpu_custom_call" | custom-call | flops 1500000000 | bytes 5000000 | tf_op jit(solution)/shard_map/swiglu_block/pallas_call | solution.py:394
  67.3 4.0 %finish.1 = (bf16[8,1024]{1,0:T(8,128)(2,1)}, bf16[8,1024]{1,0:T(8,128)(2,1)}, bf16[448,1024]{1,0:T(8,128)(2,1)}, bf16[448,1024]{1,0:T(8,128)(2,1)}) custom-call(bf16[512,1024]{1,0:T(8,128)(2,1)} %get-tuple-element.12.x_ref, bf16[512,896]{1,0:T(8,128)(2,1)} %get-tuple-element.13.g_ref, bf16[16,16,512]{2,1,0:T(8,128)(2,1)} %get-tuple-element.14.lo_ref, ...), custom_call_target="tpu_custom_call" | custom-call | flops 940000000 | bytes 4500000 | tf_op jit(solution)/shard_map/finish/pallas_call | solution.py:410

commit v4 on v3

--- a/solution.py
+++ b/solution.py
@@ -137,7 +137,6 @@
         loop(1, 16, one)
 
     spread(gx, GROUPS["tok"])
-    spread(gc, GROUPS["cot"])
 
     def unfold(buf, into, first, q):
         for core in range(2):
@@ -146,8 +145,8 @@
             into[at, :512] = jnp.concatenate([a[:8], b[:8]], axis=0).astype(BF16)
             into[at, 512:] = jnp.concatenate([a[8:], b[8:]], axis=0).astype(BF16)
 
-    def pair_up(buf, base, sib_base):
-        for half in (1, 0):
+    def pair_up(buf, base, sib_base, halves):
+        for half in halves:
             lo = 8 * half
             loop(max(lo, 1), lo + 8, lambda j: arrived(buf.at[k, j], base + j))
             mine = buf.at[k, pl.ds(lo, 8)]
@@ -172,19 +171,17 @@
     def relay(src, near, far, both, base, parity):
         @pl.when(odd_row == parity)
         def _():
-            for i in range(3):
+            for i in (1 - parity, parity, 2):
                 arrived(far.at[i], base + 4 + i)
-            third = far[2].astype(F32)
-            up_sum = src[at_row(2)].astype(F32) + far[0].astype(F32)
-            down_sum = src[at_row(-2)].astype(F32) + far[1].astype(F32)
-            if parity == 0:
-                up_sum = up_sum + third
-            else:
-                down_sum = down_sum + third
-            both[0] = up_sum.astype(BF16)
-            both[1] = down_sum.astype(BF16)
-            copy(both.at[0], near.at[2], base + 2, base + 2, row_device(2)).start()
-            copy(both.at[1], near.at[3], base + 3, base + 3, row_device(-2)).start()
+                if i == parity:
+                    continue
+                side = 1 - parity if i < 2 else parity
+                total = src[at_row(2 - 4 * side)].astype(F32) + far[side].astype(F32)
+                if i == 2:
+                    total = total + far[2].astype(F32)
+                both[side] = total.astype(BF16)
+                at = base + 2 + side
+                copy(both.at[side], near.at[2 + side], at, at, row_device(2 - 4 * side)).start()
 
     def reduce_and_share(src, near, whole, base, share):
         for i in range(4):
@@ -212,7 +209,9 @@
     def come(whole, share, lo, hi):
         loop(lo, hi, lambda i: arrived(whole.at[group_of(ring(i))], share + i))
 
-    pair_up(gx, GROUPS["tok"], GROUPS["tok_sib"])
+    pair_up(gx, GROUPS["tok"], GROUPS["tok_sib"], (1,))
+    spread(gc, GROUPS["cot"])
+    pair_up(gx, GROUPS["tok"], GROUPS["tok_sib"], (0,))
     for half in (1, 0):
         collect(gx, x, half, GROUPS["tok_sib"])
         if half == 1:
@@ -224,8 +223,9 @@
         scatter(sgu, rgu, lgu, half, GROUPS["zgu"])
     copy(gx.at[k], gp.at[k], GROUPS["px"], GROUPS["px"], peer).start()
     relay(sgu, rgu, lgu, cgu, GROUPS["zgu"], 1)
+    pair_up(gc, GROUPS["cot"], GROUPS["cot_sib"], (1,))
     relay(sgu, rgu, lgu, cgu, GROUPS["zgu"], 0)
-    pair_up(gc, GROUPS["cot"], GROUPS["cot_sib"])
+    pair_up(gc, GROUPS["cot"], GROUPS["cot_sib"], (0,))
     for half in (1, 0):
         collect(gc, cx, half, GROUPS["cot_sib"])
         if half == 1:
@@ -326,16 +326,6 @@
     loop(0, 8, lambda q: unfold(gp, x, 256, q))
     save_x = pltpu.make_async_copy(x, x_out, wsem.at[5])
     save_x.start()
-    loop(1, 16, lambda j: arrived(lo_r.at[j], GROUPS["lo"] + j))
-    save_lo = pltpu.make_async_copy(lo_r, lo_out, wsem.at[6])
-    save_lo.start()
-    loop(0, 8, lambda q: arrived(g.at[rows(256 + 32 * q, 32)], GROUPS["pg"] + q))
-    save_g = pltpu.make_async_copy(g, g_out, wsem.at[7])
-    save_g.start()
-    loop(1, 16, lambda j: arrived(gi_r.at[j], GROUPS["gi"] + j))
-    save_gi = pltpu.make_async_copy(gi_r, gi_out, wsem.at[8])
-    save_gi.start()
-
     def drain(j):
         left(gx.at[k, 0], GROUPS["tok"] + j)
         left(gc.at[k, 0], GROUPS["cot"] + j)
@@ -358,6 +348,16 @@
         left(gi_s.at[pl.ds(lo, hi - lo)], GROUPS["gi_sib"] + half)
     left(gx.at[k], GROUPS["px"])
     left(gp.at[k], GROUPS["px_sib"])
+    loop(1, 16, lambda j: arrived(lo_r.at[j], GROUPS["lo"] + j))
+    save_lo = pltpu.make_async_copy(lo_r, lo_out, wsem.at[6])
+    save_lo.start()
+    loop(0, 8, lambda q: arrived(g.at[rows(256 + 32 * q, 32)], GROUPS["pg"] + q))
+    save_g = pltpu.make_async_copy(g, g_out, wsem.at[7])
+    save_g.start()
+
+    loop(1, 16, lambda j: arrived(gi_r.at[j], GROUPS["gi"] + j))
+    save_gi = pltpu.make_async_copy(gi_r, gi_out, wsem.at[8])
+    save_gi.start()
     for save in (save_x, save_lo, save_g, save_gi):
         save.wait()
 

time: 71.6 us -> 70.5 us (0.985)
  Pallas kernels: 70.7 us -> 69.5 us
    pallas_call x1, Pallas kernels: 66.7 us -> 65.6 us  [body(): pl.pallas_call(kernel, out_shape=(jax.ShapeDtypeStruct((512, 1024), BF16)...]
where the time goes in v4:
time: 70.5 us; the launch traced here: 70.2 us
  Pallas kernels  69.5 us (99%)
    pallas_call x1, Pallas kernels, body(): pl.pallas_call(kernel, out_shape=(jax.ShapeDtypeStruct((512, 1024), BF16)...  65.6 us
    pallas_call x1, Pallas kernels, body(): pl.pallas_call(finish, out_shape=(jax.ShapeDtypeStruct((8, 1024), BF16),...  3.98 us

profile of v4, /device:TPU:1, one launch (start us, length us, event | category | flops | bytes accessed | tf_op | source)
XLA Modules:
  0.0 70.2 jit_solution(1216845596237164417)
XLA Ops:
  0.6 65.6 %swiglu_block.1 = (bf16[512,1024]{1,0:T(8,128)(2,1)}, bf16[512,896]{1,0:T(8,128)(2,1)}, bf16[16,16,512]{2,1,0:T(8,128)(2,1)}, bf16[16,16,512]{2,1,0:T(8,128)(2,1)}) custom-call(bf16[8,1024]{1,0:T(8,128)(2,1)} %tok_ref.1, bf16[448,1024]{1,0:T(8,128)(2,1)} %bitcast.4, bf16[448,1024]{1,0:T(8,128)(2,1)} %bitcast.5, bf16[448,1024]{1,0:T(8,128)(2,1)} %wd_hbm.1, ...), custom_call_target="tpu_custom_call" | custom-call | flops 1500000000 | bytes 5000000 | tf_op jit(solution)/shard_map/swiglu_block/pallas_call | solution.py:394
  66.2 4.0 %finish.1 = (bf16[8,1024]{1,0:T(8,128)(2,1)}, bf16[8,1024]{1,0:T(8,128)(2,1)}, bf16[448,1024]{1,0:T(8,128)(2,1)}, bf16[448,1024]{1,0:T(8,128)(2,1)}) custom-call(bf16[512,1024]{1,0:T(8,128)(2,1)} %get-tuple-element.12.x_ref, bf16[512,896]{1,0:T(8,128)(2,1)} %get-tuple-element.13.g_ref, bf16[16,16,512]{2,1,0:T(8,128)(2,1)} %get-tuple-element.14.lo_ref, ...), custom_call_target="tpu_custom_call" | custom-call | flops 940000000 | bytes 4500000 | tf_op jit(solution)/shard_map/finish/pallas_call | solution.py:410

commit v5 on v4

--- a/solution.py
+++ b/solution.py
@@ -221,7 +221,6 @@
         for i in range(4):
             sgu[2 * i + half] = pre[32 * i:32 * i + 32].astype(BF16)
         scatter(sgu, rgu, lgu, half, GROUPS["zgu"])
-    copy(gx.at[k], gp.at[k], GROUPS["px"], GROUPS["px"], peer).start()
     relay(sgu, rgu, lgu, cgu, GROUPS["zgu"], 1)
     pair_up(gc, GROUPS["cot"], GROUPS["cot_sib"], (1,))
     relay(sgu, rgu, lgu, cgu, GROUPS["zgu"], 0)
@@ -236,10 +235,9 @@
         scatter(sgh, rgh, lgh, half, GROUPS["zgh"])
     relay(sgh, rgh, lgh, cgh, GROUPS["zgh"], 1)
     relay(sgh, rgh, lgh, cgh, GROUPS["zgh"], 0)
+    copy(gx.at[k], gp.at[k], GROUPS["px"], GROUPS["px"], peer).start()
     reduce_and_share(sgu, rgu, agu, GROUPS["zgu"], GROUPS["agu"])
     reduce_and_share(sgh, rgh, agh, GROUPS["zgh"], GROUPS["agh"])
-    arrived(gp.at[k], GROUPS["px"])
-    copy(gp.at[k], gp.at[k], GROUPS["px_sib"], GROUPS["px_sib"], sib).start()
 
     first, last = (0, 5), (5, 8)
 
@@ -313,6 +311,8 @@
     pass_on(agh, GROUPS["agh"])
     come(agh, GROUPS["agh"], 1, 3)
     backward(0)
+    arrived(gp.at[k], GROUPS["px"])
+    copy(gp.at[k], gp.at[k], GROUPS["px_sib"], GROUPS["px_sib"], sib).start()
     to_owners(lo_f, lo_i, lo_t, lo_r, 0, "lo_sib", GROUPS["lo"])
     to_owners(gi_f, gi_i, gi_t, gi_r, 0, "gi_sib", GROUPS["gi"])
     come(agu, GROUPS["agu"], 5, 8)

time: 70.5 us -> 70.2 us (level)
  no operation moved by 1% of the time
where the time goes in v5:
time: 70.2 us; the launch traced here: 69.9 us
  Pallas kernels  69.3 us (99%)
    pallas_call x1, Pallas kernels, body(): pl.pallas_call(kernel, out_shape=(jax.ShapeDtypeStruct((512, 1024), BF16)...  65.3 us
    pallas_call x1, Pallas kernels, body(): pl.pallas_call(finish, out_shape=(jax.ShapeDtypeStruct((8, 1024), BF16),...  3.98 us

profile of v5, /device:TPU:1, one launch (start us, length us, event | category | flops | bytes accessed | tf_op | source)
XLA Modules:
  0.0 69.9 jit_solution(5082232995610043796)
XLA Ops:
  0.6 65.3 %swiglu_block.1 = (bf16[512,1024]{1,0:T(8,128)(2,1)}, bf16[512,896]{1,0:T(8,128)(2,1)}, bf16[16,16,512]{2,1,0:T(8,128)(2,1)}, bf16[16,16,512]{2,1,0:T(8,128)(2,1)}) custom-call(bf16[8,1024]{1,0:T(8,128)(2,1)} %tok_ref.1, bf16[448,1024]{1,0:T(8,128)(2,1)} %bitcast.4, bf16[448,1024]{1,0:T(8,128)(2,1)} %bitcast.5, bf16[448,1024]{1,0:T(8,128)(2,1)} %wd_hbm.1, ...), custom_call_target="tpu_custom_call" | custom-call | flops 1500000000 | bytes 5000000 | tf_op jit(solution)/shard_map/swiglu_block/pallas_call | solution.py:394
  65.9 4.0 %finish.1 = (bf16[8,1024]{1,0:T(8,128)(2,1)}, bf16[8,1024]{1,0:T(8,128)(2,1)}, bf16[448,1024]{1,0:T(8,128)(2,1)}, bf16[448,1024]{1,0:T(8,128)(2,1)}) custom-call(bf16[512,1024]{1,0:T(8,128)(2,1)} %get-tuple-element.12.x_ref, bf16[512,896]{1,0:T(8,128)(2,1)} %get-tuple-element.13.g_ref, bf16[16,16,512]{2,1,0:T(8,128)(2,1)} %get-tuple-element.14.lo_ref, ...), custom_call_target="tpu_custom_call" | custom-call | flops 940000000 | bytes 4500000 | tf_op jit(solution)/shard_map/finish/pallas_call | solution.py:410
